TPU v7x, 32 devices: a whole 2x2x4 slice. The times are simulated.
32 devices in a mesh: scen: 16 (over z, y, x), sub: 2 (over core).
Axes of the slice: x: 2, y: 2, z: 4, core: 2. Of those that a mesh axis runs over, the one named last changes fastest.
Arguments:
- disturbance: float32 [8, 32, 48, 2048], P('sub', None, None, 'scen'), may hold values from -6 to 6
- prior_states: float32 [8, 32, 48, 2048], P('sub', None, None, 'scen'), may hold values from -6 to 6
- initial_state: float32 [8, 48], P('sub'), may hold values from -6 to 6
- scaled_duals: float32 [8, 7, 16, 2048], P('sub', None, None, 'scen'), may hold values from -3 to 3
- dynamics: float32 [8, 48, 48], P('sub'), may hold values from -0.5 to 0.5
- actuation: float32 [8, 48, 16], P('sub'), may hold values from -0.4375 to 0.4375
- cost_to_go: float32 [8, 32, 48, 48], P('sub'), may hold values from -0.875 to 0.875
- inverses: float32 [8, 32, 16, 16], P('sub'), may hold values from -0.75 to 0.75
- couplers: float32 [8, 2, 48, 48], replicated, may hold values from -0.625 to 0.625
- neighbours: int32 [8, 2], replicated, may hold values from 0 to 7, as said below
- branches: int32 [6, 2048], P(None, 'scen'), may hold values from 0 to 1, as said below
Outputs:
- states: float32 [8, 32, 48, 2048], P('sub', None, None, 'scen')
- controls: float32 [8, 32, 16, 2048], P('sub', None, None, 'scen')
- new_duals: float32 [8, 7, 16, 2048], P('sub', None, None, 'scen')
Inputs may be any that keep to these rules, and one draw needn't show every extreme that they name: For every t from 0 to 6, the scenarios that agree on branches 0 to t - 1 number exactly 2048 / 2^t. `neighbours`: each row names 2 different subsystems, none of them the row's own.
All inputs are finite; a program needn't handle non-finite values.
Results may differ from a plain program's by a relative error of at most 0.0001.
Values sent between devices are 32-bit elements; how exact they have to be, the bound alone decides.
A program may use at most 128 MiB of HBM per device.

v0:
```python
import functools

import jax
import jax.numpy as jnp
from jax import lax
from jax.experimental import pallas as pl
from jax.experimental.pallas import tpu as pltpu
from jax.sharding import PartitionSpec as P

SWEEPS = 2
F32, BF16 = jnp.float32, jnp.bfloat16
VMEM_BYTES = 56 * 1024 * 1024


def exact_dot(a, b):
    return jnp.dot(a, b, precision=lax.Precision.HIGHEST, preferred_element_type=F32)


def halves(x):
    hi = x.astype(BF16)
    return hi, (x - hi.astype(F32)).astype(BF16)


def wide(w):
    hi, lo = halves(w)
    return jnp.concatenate([hi.astype(F32), lo.astype(F32), hi.astype(F32)], axis=1).astype(BF16)


def tall(x):
    hi, lo = halves(x)
    return jnp.concatenate([hi, hi, lo], axis=0)


def mxu(a, b):
    return jnp.dot(a, b, preferred_element_type=F32)


def prepare(t, dyn, act, ctg, inv, wb, wf, wp, dyn_t, act_t):
    subs = dyn.shape[0]
    for m in range(subs):
        a, b, at, bt = dyn[m], act[m], dyn_t[m], act_t[m]
        p, g = ctg[m, t], inv[m, t]
        gain = -exact_dot(g, exact_dot(exact_dot(bt, p), a))
        closed = a + exact_dot(b, gain)
        back = -exact_dot(g, bt)
        bg = -exact_dot(b, g)
        left = jnp.concatenate([closed.T, back, exact_dot(b, back)], axis=0)
        right = jnp.concatenate([gain.T, -g, bg], axis=0)
        wb[m, t] = jnp.concatenate([wide(left).astype(F32), wide(right).astype(F32)], axis=1).astype(BF16)
        wf[m, t] = wide(jnp.concatenate([closed, gain], axis=0))
        wp[m, t] = wide(p)


def couple(own_first, other_first, neigh, coup, cx):
    subs, nb, nx, ncp = coup.shape
    for side, first in enumerate((own_first, other_first)):
        for i in range(subs):
            for j in range(subs):
                total = jnp.zeros((nx, ncp), F32)
                for e in range(nb):
                    hit = neigh[i, e] == first + j
                    total = total + jnp.where(hit, coup[i, e], 0.0)
                hi, lo = halves(total)
                at = (side * subs + j) * ncp
                cx[0, i * nx:(i + 1) * nx, at:at + ncp] = hi
                cx[1, i * nx:(i + 1) * nx, at:at + ncp] = lo


def influence(t, own, other, cx):
    subs = own.shape[0]
    blocks = [own[j, t] for j in range(subs)] + [other[j, t] for j in range(subs)]
    x = jnp.concatenate(blocks, axis=0)
    hi, lo = halves(x)
    return mxu(cx[0], hi) + mxu(cx[1], hi) + mxu(cx[0], lo)


def sweep(own, other, dist, linear, init, wb, wf, wp, cx, drive, offs, states, controls):
    subs, steps, nx, s = dist.shape
    nu = controls.shape[2]
    robust = linear.shape[1]

    def grow(t):
        flow = influence(t, own, other, cx)
        out = []
        for i in range(subs):
            d = dist[i, t] + flow[i * nx:(i + 1) * nx]
            drive[i, t] = d
            out.append(mxu(wp[i, t], tall(d)))
        return tuple(out)

    def back(t, carry, with_linear):
        costate, q = carry
        ahead = grow(jnp.maximum(t - 1, 0))
        after = []
        for i in range(subs):
            right = tall(q[i] + costate[i])
            if with_linear:
                right = jnp.concatenate([right, tall(linear[i, t])], axis=0)
                y = mxu(wb[i, t], right)
            else:
                y = mxu(wb[i, t, :, :3 * nx], right)
            offs[i, t] = y[nx:nx + nu]
            states[i, t] = y[nx + nu:]
            after.append(y[:nx])
        return tuple(after), ahead

    zero = tuple(jnp.zeros((nx, s), F32) for _ in range(subs))
    carry = (zero, grow(steps - 1))
    carry = lax.fori_loop(0, steps - robust, lambda k, c: back(steps - 1 - k, c, False), carry)
    carry = lax.fori_loop(0, robust, lambda k, c: back(robust - 1 - k, c, True), carry)

    def ahead(t, x):
        after = []
        for i in range(subs):
            y = mxu(wf[i, t], tall(x[i]))
            controls[i, t] = y[nx:] + offs[i, t]
            now = y[:nx] + (states[i, t] + drive[i, t])
            states[i, t] = now
            after.append(now)
        return tuple(after)

    x = tuple(jnp.broadcast_to(init[i], (nx, s)) for i in range(subs))
    return ahead, x


def member(t, ids, lanes):
    s = ids.shape[1]
    place = lax.broadcasted_iota(jnp.int32, (lanes, s), 0)
    return jnp.where(place == ids[t:t + 1, :] + (2**t - 1), 1.0, 0.0).astype(BF16)


def node_sums(averaged, ids, lanes):
    robust = len(averaged)
    total = None
    for t in range(robust):
        hot = member(t, ids, lanes)
        for part in halves(averaged[t]):
            term = lax.dot_general(part, hot, (((1,), (1,)), ((), ())), preferred_element_type=F32)
            total = term if total is None else total + term
    return total


def node_means(totals, robust, scen_total):
    place = lax.broadcasted_iota(jnp.int32, totals.shape, 1)
    shares = jnp.ones(totals.shape, F32)
    for t in range(1, robust):
        shares = jnp.where(place >= 2**t - 1, float(2**t), shares)
    return totals * (shares / float(scen_total))


def spread(means, t, ids):
    hot = member(t, ids, means.shape[1])
    hi, lo = halves(means)
    return mxu(hi, hot) + mxu(lo, hot)


def gathered(controls, duals, t):
    subs = duals.shape[0]
    return jnp.concatenate([controls[i, t] + duals[i, t] for i in range(subs)], axis=0)


def first_kernel(firsts, neigh, own, other, dist, duals, init, dyn, act, ctg, inv, coup, ids,
                 states, controls, sums, wb, wf, wp, cx, drive, offs, dyn_t, act_t):
    subs, robust = duals.shape[:2]
    steps = dist.shape[1]
    for m in range(subs):
        dyn_t[m] = dyn[m].T
        act_t[m] = act[m].T
    couple(firsts[0], firsts[1], neigh, coup, cx)

    def prep(t, c):
        prepare(t, dyn, act, ctg, inv, wb, wf, wp, dyn_t, act_t)
        return c

    lax.fori_loop(0, steps, prep, 0)
    step, x = sweep(own, other, dist, duals, init, wb, wf, wp, cx, drive, offs, states, controls)
    lax.fori_loop(0, steps, step, x)
    ids_now = ids[...]
    averaged = [gathered(controls, duals, t) for t in range(robust)]
    sums[...] = node_sums(averaged, ids_now, sums.shape[1])


def second_kernel(scen_total, own, other, dist, duals, init, before, ids, totals, wb, wf, wp, cx,
                  states, controls, sums, averaged_out, drive, offs, linear, duals_now):
    subs, robust, nu, s = duals.shape
    steps = dist.shape[1]
    ids_now = ids[...]
    means = node_means(totals[...], robust, scen_total)
    for t in range(robust):
        consensus = spread(means, t, ids_now)
        for i in range(subs):
            c = consensus[i * nu:(i + 1) * nu]
            now = duals[i, t] + before[i, t] - c
            duals_now[i, t] = now
            linear[i, t] = now - c
    step, x = sweep(own, other, dist, linear, init, wb, wf, wp, cx, drive, offs, states, controls)
    lax.fori_loop(0, steps, step, x)
    averaged = []
    for t in range(robust):
        v = gathered(controls, duals_now, t)
        averaged.append(v)
        for i in range(subs):
            averaged_out[i, t] = v[i * nu:(i + 1) * nu]
    sums[...] = node_sums(averaged, ids_now, sums.shape[1])


def last_kernel(scen_total, averaged, ids, totals, out):
    subs, robust, nu, s = averaged.shape
    means = node_means(totals[...], robust, scen_total)
    for t in range(robust):
        consensus = spread(means, t, ids[...])
        for i in range(subs):
            out[i, t] = averaged[i, t] - consensus[i * nu:(i + 1) * nu]


def shards(mesh, disturbance, prior_states, initial_state, scaled_duals, dynamics, actuation, cost_to_go,
           inverses, couplers, neighbours, branches):
    subs, steps, nx, s = disturbance.shape
    robust, nu = scaled_duals.shape[1:3]
    ncp = prior_states.shape[2]
    n_scen, n_sub = mesh.shape["scen"], mesh.shape["sub"]
    scen_total = s * n_scen
    me = lax.axis_index("sub")
    first = me * subs
    other_first = ((me + 1) % n_sub) * subs
    swap = [((k + 1) % n_sub, k) for k in range(n_sub)]
    coup = lax.dynamic_slice_in_dim(couplers, first, subs, 0)
    neigh = lax.dynamic_slice_in_dim(neighbours, first, subs, 0)
    firsts = jnp.stack([first, other_first]).astype(jnp.int32)
    rows = [jnp.zeros((s,), jnp.int32)]
    for k in range(branches.shape[0]):
        rows.append(rows[-1] + branches[k] * 2**k)
    ids = jnp.stack(rows)
    lanes = 2**robust
    init = initial_state[:, :, None]

    vm, sm = pl.BlockSpec(memory_space=pltpu.VMEM), pl.BlockSpec(memory_space=pltpu.SMEM)
    big = jax.ShapeDtypeStruct((subs, steps, nx, s), F32)
    small = jax.ShapeDtypeStruct((subs, steps, nu, s), F32)
    sums = jax.ShapeDtypeStruct((subs * nu, lanes), F32)
    few = jax.ShapeDtypeStruct((subs, robust, nu, s), F32)
    weights = [
        jax.ShapeDtypeStruct((subs, steps, 2 * nx + nu, 3 * (nx + nu)), BF16),
        jax.ShapeDtypeStruct((subs, steps, nx + nu, 3 * nx), BF16),
        jax.ShapeDtypeStruct((subs, steps, nx, 3 * nx), BF16),
        jax.ShapeDtypeStruct((2, subs * nx, 2 * subs * ncp), BF16),
    ]
    params = pltpu.CompilerParams(vmem_limit_bytes=VMEM_BYTES)
    scratch = [pltpu.VMEM((subs, steps, nx, s), F32), pltpu.VMEM((subs, steps, nu, s), F32)]
    other = lax.ppermute(prior_states, "sub", swap)
    states, controls, partial, *made = pl.pallas_call(
        first_kernel,
        out_shape=[big, small, sums] + weights,
        in_specs=[sm, sm] + [vm] * 11,
        out_specs=[vm] * 7,
        scratch_shapes=scratch + [pltpu.VMEM((subs, nx, nx), F32), pltpu.VMEM((subs, nu, nx), F32)],
        compiler_params=params,
    )(firsts, neigh, prior_states, other, disturbance, scaled_duals, init, dynamics, actuation,
      cost_to_go, inverses, coup, ids)
    other = lax.ppermute(states[:, :, :ncp], "sub", swap)
    totals = lax.psum(partial, "scen")
    states, controls, partial, averaged = pl.pallas_call(
        functools.partial(second_kernel, scen_total),
        out_shape=[big, small, sums, few],
        in_specs=[vm] * 12,
        out_specs=[vm] * 4,
        scratch_shapes=scratch + [pltpu.VMEM(few.shape, F32), pltpu.VMEM(few.shape, F32)],
        compiler_params=params,
    )(states, other, disturbance, scaled_duals, init, controls[:, :robust], ids, totals, *made)
    totals = lax.psum(partial, "scen")
    new_duals = pl.pallas_call(
        functools.partial(last_kernel, scen_total),
        out_shape=few,
        in_specs=[vm] * 3,
        out_specs=vm,
        compiler_params=params,
    )(averaged, ids, totals)
    return states, controls, new_duals


def solution(mesh):
    wide_spec = P("sub", None, None, "scen")
    placed = (wide_spec, wide_spec, P("sub", None), wide_spec, P("sub", None, None), P("sub", None, None),
              P("sub", None, None, None), P("sub", None, None, None), P(), P(), P(None, "scen"))
    return jax.shard_map(
        functools.partial(shards, mesh), mesh=mesh, in_specs=placed, out_specs=(wide_spec,) * 3,
        check_vma=False,
    )
```

profile of v0, /device:TPU:0, one launch (start us, length us, event | category | flops | bytes accessed | tf_op | source)
XLA Modules:
  0.0 304.6 jit_solution(6700659906393468733)
XLA Ops:
  0.6 0.0 copy-start
  0.6 0.5 collective-permute-start
  1.2 0.7 constant_dynamic-slice_fusion.1
  1.9 0.7 copy.22.neigh
  2.6 1.4 copy.18.init
  4.0 1.5 copy.19.act
  5.5 2.4 copy.20.inv
  7.9 1.5 multiply_add_fusion
  9.4 0.6 stack_broadcast_in_dim.3
  10.0 1.3 stack.20.ids
  11.3 0.6 pad_add_fusion.firsts
  11.9 0.0 copy-done
  11.9 0.7 constant_dynamic-slice_fusion.coup
  12.6 0.0 collective-permute-done.other
  12.6 0.0 copy-start.1
  12.6 1.7 copy-done.1
  14.3 100.2 %shard_map.130 = (f32[4,32,48,128]{3,2,1,0:T(8,128)}, f32[4,32,16,128]{3,2,1,0:T(8,128)}, f32[64,128]{1,0:T(8,128)}, bf16[4,32,112,192]{3,2,1,0:T(8,128)(2,1)}, ...) custom-call(s32[2]{0:T(128)} %pad_add_fusion.firsts, ...), custom_call_target="tpu_custom_call" | custom-call | tf_op jit(solution)/shard_map/pallas_call | solution.py:251
  114.5 0.1 collective-permute-start.1
  114.5 1.6 slice.27.before
  116.2 79.1 %psum.14.totals = f32[64,128]{1,0:T(8,128)} all-reduce(f32[64,128]{1,0:T(8,128)} %get-tuple-element.16), channel_id=1, replica_groups=mesh['scen'=16,'sub'=2] {'scen'}, use_global_device_ids=true, to_apply=%region_0.1 | all-reduce | flops 8192 | bytes 65536 | tf_op jit(solution)/shard_map/psum | solution.py:261
  195.3 0.0 collective-permute-done.1.other
  195.3 0.0 copy-start.2
  195.3 1.6 copy-done.2
  196.9 33.1 %shard_map.131 = (f32[4,32,48,128]{3,2,1,0:T(8,128)}, f32[4,32,16,128]{3,2,1,0:T(8,128)}, f32[64,128]{1,0:T(8,128)}, f32[4,7,16,128]{3,2,1,0:T(8,128)}) custom-call(f32[4,32,48,128]{3,2,1,0:T(8,128)} %get-tuple-element.14.own, f32[4,32,48,128]{3,2,1,0:T(8,128)} %copy-done.2, f32[4,32,48,128]{3,2,1,0:T(8,128)} %dist.3, f32[4,7,16,128]{3,2,1,0:T(8,128)} %duals.3, ...), custom_call_target="tpu_custom_call" | custom-call | tf_op jit(solution)/shard_map/pallas_call | solution.py:262
  230.0 72.6 %psum.15.totals = f32[64,128]{1,0:T(8,128)} all-reduce(f32[64,128]{1,0:T(8,128)} %get-tuple-element.24), channel_id=1, replica_groups=mesh['scen'=16,'sub'=2] {'scen'}, use_global_device_ids=true, to_apply=%region_1.2 | all-reduce | flops 8192 | bytes 65536 | tf_op jit(solution)/shard_map/psum | solution.py:270
  302.6 1.9 shard_map.132
Async XLA Ops:
  0.6 11.3 %copy-start = (f32[8,2,48,48]{3,2,1,0:T(8,128)S(1)}, f32[8,2,48,48]{3,2,1,0:T(8,128)}, u32[]{:S(2)}) copy-start(f32[8,2,48,48]{3,2,1,0:T(8,128)} %param.19) | copy-start | bytes 442372
  0.6 12.0 %collective-permute-start = (f32[4,32,48,128]{3,2,1,0:T(8,128)}, f32[4,32,48,128]{3,2,1,0:T(8,128)S(1)}, u32[]{:S(2)}, u32[]{:S(2)}) collective-permute-start(f32[4,32,48,128]{3,2,1,0:T(8,128)} %own.1), channel_id=1, source_target_pairs={{1,0},{0,1},{3,2},{2,3},{5,4},{4,5},{7,6},{6,7},{9,8},{8,9},{11,10... | collective-permute-start | bytes 9437192 | tf_op jit(solution)/shard_map/ppermute | solution.py:250
  12.6 1.7 copy-start.1
  114.5 80.8 %collective-permute-start.1 = (f32[4,32,48,128]{3,2,1,0:T(8,128)}, f32[4,32,48,128]{3,2,1,0:T(8,128)S(1)}, u32[]{:S(2)}, u32[]{:S(2)}) collective-permute-start(f32[4,32,48,128]{3,2,1,0:T(8,128)} %get-tuple-element.14.own), channel_id=1, source_target_pairs={{1,0},{0,1},{3,2},{2,3},{5,4},{4,5},{7,6},{6,7},{9,8},{8,9},{11,10... | collective-permute-start | bytes 9437192 | tf_op jit(solution)/shard_map/ppermute | solution.py:260
  195.3 1.6 copy-start.2
where the time goes:
time: 305 us
  blocking collectives  152 us (50%)
  Pallas kernels  135 us (44%)
  local copies, waits for them, and re-layouts  14.2 us (5%)
    psum x2, blocking collectives, shards(): totals = lax.psum(partial, 'scen')  152 us
    pallas_call x1, Pallas kernels, shards(): pl.pallas_call(first_kernel, out_shape=[big, small, sums] + weights, in_s...  100 us
    pallas_call x1, Pallas kernels, shards(): pl.pallas_call(functools.partial(second_kernel, scen_total), out_shape=[b...  33.1 us
    unnamed x9, local copies, waits for them, and re-layouts  7.88 us
  transfers between devices with their start and end apart: 2, of which 0 were waited for; matrix products, arithmetic and copies ran while one was open for 4% of the time, Pallas kernels for 0%

commit v1 on v0

--- a/solution.py
+++ b/solution.py
@@ -12,10 +12,6 @@
 VMEM_BYTES = 56 * 1024 * 1024
 
 
-def exact_dot(a, b):
-    return jnp.dot(a, b, precision=lax.Precision.HIGHEST, preferred_element_type=F32)
-
-
 def halves(x):
     hi = x.astype(BF16)
     return hi, (x - hi.astype(F32)).astype(BF16)
@@ -35,31 +31,45 @@
     return jnp.dot(a, b, preferred_element_type=F32)
 
 
-def prepare(t, dyn, act, ctg, inv, wb, wf, wp, dyn_t, act_t):
-    subs = dyn.shape[0]
-    for m in range(subs):
-        a, b, at, bt = dyn[m], act[m], dyn_t[m], act_t[m]
-        p, g = ctg[m, t], inv[m, t]
-        gain = -exact_dot(g, exact_dot(exact_dot(bt, p), a))
-        closed = a + exact_dot(b, gain)
-        back = -exact_dot(g, bt)
-        bg = -exact_dot(b, g)
-        left = jnp.concatenate([closed.T, back, exact_dot(b, back)], axis=0)
-        right = jnp.concatenate([gain.T, -g, bg], axis=0)
-        wb[m, t] = jnp.concatenate([wide(left).astype(F32), wide(right).astype(F32)], axis=1).astype(BF16)
-        wf[m, t] = wide(jnp.concatenate([closed, gain], axis=0))
-        wp[m, t] = wide(p)
-
-
-def couple(own_first, other_first, neigh, coup, cx):
-    subs, nb, nx, ncp = coup.shape
+def dot3(a, b):
+    a_hi, a_lo = halves(a)
+    b_hi, b_lo = halves(b)
+    return mxu(a_hi, b_hi) + (mxu(a_lo, b_hi) + mxu(a_hi, b_lo))
+
+
+def prepare(times, dyn, act_t, ctg, inv, wb, wf, wp):
+    subs, nx = dyn.shape[:2]
+    nu = act_t.shape[1]
+    work = [(m, t) for t in times for m in range(subs)]
+    bt = [act_t[m] for m in range(subs)]
+    at = [tall(dyn[m]) for m in range(subs)]
+    pa = []
+    for m, t in work:
+        p = wide(ctg[m, t])
+        wp[m, t] = p
+        pa.append(mxu(p, at[m]))
+    g = [inv[m, t] for m, t in work]
+    bg = [dot3(bt[m].T, g[k]) for k, (m, t) in enumerate(work)]
+    x2 = [dot3(bt[m], pa[k]) for k, (m, t) in enumerate(work)]
+    both = [-jnp.concatenate([g[k], bg[k]], axis=0) for k in range(len(work))]
+    low = [dot3(both[k], bt[m]) for k, (m, t) in enumerate(work)]
+    gain = [dot3(both[k], x2[k]) for k in range(len(work))]
+    for k, (m, t) in enumerate(work):
+        front = jnp.concatenate([dyn[m] + gain[k][nu:], gain[k][:nu]], axis=0)
+        wf[m, t] = wide(front)
+        bottom = jnp.concatenate([low[k], both[k]], axis=1)
+        wb[m, t] = wide(jnp.concatenate([front.T, bottom], axis=0))
+
+
+def couple(subs, own_first, other_first, neigh, coup, cx):
+    nb, nx, ncp = coup.shape[1:]
     for side, first in enumerate((own_first, other_first)):
         for i in range(subs):
             for j in range(subs):
                 total = jnp.zeros((nx, ncp), F32)
                 for e in range(nb):
-                    hit = neigh[i, e] == first + j
-                    total = total + jnp.where(hit, coup[i, e], 0.0)
+                    hit = neigh[e, own_first + i] == first + j
+                    total = total + jnp.where(hit, coup[own_first + i, e], 0.0)
                 hi, lo = halves(total)
                 at = (side * subs + j) * ncp
                 cx[0, i * nx:(i + 1) * nx, at:at + ncp] = hi
@@ -93,12 +103,8 @@
         ahead = grow(jnp.maximum(t - 1, 0))
         after = []
         for i in range(subs):
-            right = tall(q[i] + costate[i])
-            if with_linear:
-                right = jnp.concatenate([right, tall(linear[i, t])], axis=0)
-                y = mxu(wb[i, t], right)
-            else:
-                y = mxu(wb[i, t, :, :3 * nx], right)
+            push = linear[i, t] if with_linear else jnp.zeros((nu, s), F32)
+            y = mxu(wb[i, t], tall(jnp.concatenate([q[i] + costate[i], push], axis=0)))
             offs[i, t] = y[nx:nx + nu]
             states[i, t] = y[nx + nu:]
             after.append(y[:nx])
@@ -119,7 +125,7 @@
             after.append(now)
         return tuple(after)
 
-    x = tuple(jnp.broadcast_to(init[i], (nx, s)) for i in range(subs))
+    x = tuple(jnp.broadcast_to(init[...].T[:, i:i + 1], (nx, s)) for i in range(subs))
     return ahead, x
 
 
@@ -127,6 +133,74 @@
     s = ids.shape[1]
     place = lax.broadcasted_iota(jnp.int32, (lanes, s), 0)
     return jnp.where(place == ids[t:t + 1, :] + (2**t - 1), 1.0, 0.0).astype(BF16)
+
+
+def node_ids(branches):
+    rows = [jnp.zeros((1, branches.shape[1]), jnp.int32)]
+    for k in range(branches.shape[0]):
+        rows.append(rows[-1] + branches[k:k + 1] * 2**k)
+    return jnp.concatenate(rows, axis=0)
+
+
+def put(sums, values):
+    count, rows, lanes = sums.shape
+    extra = count * rows - values.shape[0]
+    if extra:
+        values = jnp.concatenate([values, jnp.zeros((extra, lanes), F32)], axis=0)
+    for k in range(count):
+        sums[k] = values[k * rows:(k + 1) * rows]
+
+
+def take(totals, rows):
+    return jnp.concatenate([totals[k] for k in range(-(-rows // totals.shape[1]))], axis=0)[:rows]
+
+
+def reduce_kernel(part, out, land, full, send_a, recv_a, send_b, recv_b):
+    n = part.shape[0]
+    me = lax.axis_index("scen")
+    barrier = pltpu.get_barrier_semaphore()
+
+    def over(step):
+        def body(k, c):
+            step(k, lax.rem(me + k, n))
+            return c
+
+        lax.fori_loop(1, n, body, 0)
+
+    def piece(k, to):
+        return pltpu.make_async_remote_copy(
+            src_ref=part.at[to], dst_ref=land.at[k], send_sem=send_a.at[k], recv_sem=recv_a.at[k],
+            device_id={"scen": to}, device_id_type=pl.DeviceIdType.MESH)
+
+    def whole(k, to):
+        return pltpu.make_async_remote_copy(
+            src_ref=full.at[me], dst_ref=full.at[me], send_sem=send_b.at[k], recv_sem=recv_b.at[k],
+            device_id={"scen": to}, device_id_type=pl.DeviceIdType.MESH)
+
+    over(lambda k, to: pl.semaphore_signal(
+        barrier, inc=1, device_id={"scen": to}, device_id_type=pl.DeviceIdType.MESH))
+    pl.semaphore_wait(barrier, n - 1)
+    over(lambda k, to: piece(k, to).start())
+    over(lambda k, to: piece(k, to).wait_recv())
+    full[me] = lax.fori_loop(1, n, lambda k, c: c + land[k], part[me])
+    over(lambda k, to: whole(k, to).start())
+    over(lambda k, to: piece(k, to).wait_send())
+    over(lambda k, to: whole(k, to).wait_recv())
+    over(lambda k, to: whole(k, to).wait_send())
+    out[...] = full[...]
+
+
+def all_sum(part):
+    n = part.shape[0]
+    vm = pl.BlockSpec(memory_space=pltpu.VMEM)
+    return pl.pallas_call(
+        reduce_kernel,
+        out_shape=jax.ShapeDtypeStruct(part.shape, F32),
+        in_specs=[vm],
+        out_specs=vm,
+        scratch_shapes=[pltpu.VMEM(part.shape, F32)] * 2 + [pltpu.SemaphoreType.DMA((n,))] * 4,
+        compiler_params=pltpu.CompilerParams(collective_id=0, has_side_effects=True),
+    )(part)
 
 
 def node_sums(averaged, ids, lanes):
@@ -159,33 +233,32 @@
     return jnp.concatenate([controls[i, t] + duals[i, t] for i in range(subs)], axis=0)
 
 
-def first_kernel(firsts, neigh, own, other, dist, duals, init, dyn, act, ctg, inv, coup, ids,
-                 states, controls, sums, wb, wf, wp, cx, drive, offs, dyn_t, act_t):
+def first_kernel(neigh, own, other, dist, duals, init, dyn, act_t, ctg, inv, coup, branches,
+                 states, controls, sums, wb, wf, wp, cx, drive, offs):
     subs, robust = duals.shape[:2]
     steps = dist.shape[1]
-    for m in range(subs):
-        dyn_t[m] = dyn[m].T
-        act_t[m] = act[m].T
-    couple(firsts[0], firsts[1], neigh, coup, cx)
-
-    def prep(t, c):
-        prepare(t, dyn, act, ctg, inv, wb, wf, wp, dyn_t, act_t)
+    n_sub = coup.shape[0] // subs
+    me = lax.axis_index("sub")
+    couple(subs, me * subs, lax.rem(me + 1, n_sub) * subs, neigh, coup, cx)
+    each = 2 if steps % 2 == 0 else 1
+
+    def prep(k, c):
+        prepare([k * each + r for r in range(each)], dyn, act_t, ctg, inv, wb, wf, wp)
         return c
 
-    lax.fori_loop(0, steps, prep, 0)
+    lax.fori_loop(0, steps // each, prep, 0)
     step, x = sweep(own, other, dist, duals, init, wb, wf, wp, cx, drive, offs, states, controls)
     lax.fori_loop(0, steps, step, x)
-    ids_now = ids[...]
     averaged = [gathered(controls, duals, t) for t in range(robust)]
-    sums[...] = node_sums(averaged, ids_now, sums.shape[1])
-
-
-def second_kernel(scen_total, own, other, dist, duals, init, before, ids, totals, wb, wf, wp, cx,
+    put(sums, node_sums(averaged, node_ids(branches[...]), sums.shape[2]))
+
+
+def second_kernel(scen_total, own, other, dist, duals, init, before, branches, totals, wb, wf, wp, cx,
                   states, controls, sums, averaged_out, drive, offs, linear, duals_now):
     subs, robust, nu, s = duals.shape
     steps = dist.shape[1]
-    ids_now = ids[...]
-    means = node_means(totals[...], robust, scen_total)
+    ids_now = node_ids(branches[...])
+    means = node_means(take(totals, subs * nu), robust, scen_total)
     for t in range(robust):
         consensus = spread(means, t, ids_now)
         for i in range(subs):
@@ -201,14 +274,15 @@
         averaged.append(v)
         for i in range(subs):
             averaged_out[i, t] = v[i * nu:(i + 1) * nu]
-    sums[...] = node_sums(averaged, ids_now, sums.shape[1])
-
-
-def last_kernel(scen_total, averaged, ids, totals, out):
+    put(sums, node_sums(averaged, ids_now, sums.shape[2]))
+
+
+def last_kernel(scen_total, averaged, branches, totals, out):
     subs, robust, nu, s = averaged.shape
-    means = node_means(totals[...], robust, scen_total)
+    ids_now = node_ids(branches[...])
+    means = node_means(take(totals, subs * nu), robust, scen_total)
     for t in range(robust):
-        consensus = spread(means, t, ids[...])
+        consensus = spread(means, t, ids_now)
         for i in range(subs):
             out[i, t] = averaged[i, t] - consensus[i * nu:(i + 1) * nu]
 
@@ -220,24 +294,13 @@
     ncp = prior_states.shape[2]
     n_scen, n_sub = mesh.shape["scen"], mesh.shape["sub"]
     scen_total = s * n_scen
-    me = lax.axis_index("sub")
-    first = me * subs
-    other_first = ((me + 1) % n_sub) * subs
     swap = [((k + 1) % n_sub, k) for k in range(n_sub)]
-    coup = lax.dynamic_slice_in_dim(couplers, first, subs, 0)
-    neigh = lax.dynamic_slice_in_dim(neighbours, first, subs, 0)
-    firsts = jnp.stack([first, other_first]).astype(jnp.int32)
-    rows = [jnp.zeros((s,), jnp.int32)]
-    for k in range(branches.shape[0]):
-        rows.append(rows[-1] + branches[k] * 2**k)
-    ids = jnp.stack(rows)
     lanes = 2**robust
-    init = initial_state[:, :, None]
 
     vm, sm = pl.BlockSpec(memory_space=pltpu.VMEM), pl.BlockSpec(memory_space=pltpu.SMEM)
     big = jax.ShapeDtypeStruct((subs, steps, nx, s), F32)
     small = jax.ShapeDtypeStruct((subs, steps, nu, s), F32)
-    sums = jax.ShapeDtypeStruct((subs * nu, lanes), F32)
+    sums = jax.ShapeDtypeStruct((n_scen, -(-subs * nu // n_scen), lanes), F32)
     few = jax.ShapeDtypeStruct((subs, robust, nu, s), F32)
     weights = [
         jax.ShapeDtypeStruct((subs, steps, 2 * nx + nu, 3 * (nx + nu)), BF16),
@@ -251,14 +314,14 @@
     states, controls, partial, *made = pl.pallas_call(
         first_kernel,
         out_shape=[big, small, sums] + weights,
-        in_specs=[sm, sm] + [vm] * 11,
+        in_specs=[sm] + [vm] * 11,
         out_specs=[vm] * 7,
-        scratch_shapes=scratch + [pltpu.VMEM((subs, nx, nx), F32), pltpu.VMEM((subs, nu, nx), F32)],
+        scratch_shapes=scratch,
         compiler_params=params,
-    )(firsts, neigh, prior_states, other, disturbance, scaled_duals, init, dynamics, actuation,
-      cost_to_go, inverses, coup, ids)
+    )(neighbours.T, prior_states, other, disturbance, scaled_duals, initial_state, dynamics,
+      jnp.swapaxes(actuation, 1, 2), cost_to_go, inverses, couplers, branches)
     other = lax.ppermute(states[:, :, :ncp], "sub", swap)
-    totals = lax.psum(partial, "scen")
+    totals = all_sum(partial)
     states, controls, partial, averaged = pl.pallas_call(
         functools.partial(second_kernel, scen_total),
         out_shape=[big, small, sums, few],
@@ -266,15 +329,15 @@
         out_specs=[vm] * 4,
         scratch_shapes=scratch + [pltpu.VMEM(few.shape, F32), pltpu.VMEM(few.shape, F32)],
         compiler_params=params,
-    )(states, other, disturbance, scaled_duals, init, controls[:, :robust], ids, totals, *made)
-    totals = lax.psum(partial, "scen")
+    )(states, other, disturbance, scaled_duals, initial_state, controls[:, :robust], branches, totals, *made)
+    totals = all_sum(partial)
     new_duals = pl.pallas_call(
         functools.partial(last_kernel, scen_total),
         out_shape=few,
         in_specs=[vm] * 3,
         out_specs=vm,
         compiler_params=params,
-    )(averaged, ids, totals)
+    )(averaged, branches, totals)
     return states, controls, new_duals
 
 

time: 305 us -> 130 us (0.43)
  blocking collectives: 152 us -> 0 us
  Pallas kernels: 135 us -> 117 us
  local copies, waits for them, and re-layouts: 14.2 us -> 7.34 us
  waiting for transfers between devices: 0.01 us -> 3.07 us
    psum x2 -> x0, blocking collectives: 152 us -> none  [shards(): totals = lax.psum(partial, 'scen')]
    pallas_call x1, Pallas kernels: 100 us -> 52.2 us  [shards(): pl.pallas_call(first_kernel, out_shape=[big, small, sums] + weights, in_s...]
    pallas_call x0 -> x2, Pallas kernels: none -> 29.7 us  [all_sum(): pl.pallas_call(reduce_kernel, out_shape=jax.ShapeDtypeStruct(part.shape,...]
    ppermute x1, waiting for transfers between devices: 0.01 us -> 3.06 us  [shards(): other = lax.ppermute(prior_states, 'sub', swap)]
    unnamed x9 -> x5, local copies, waits for them, and re-layouts: 7.88 us -> 5.7 us
  transfers between devices with their start and end apart: 2 -> 2, of which waited for: 0 -> 1; matrix products, arithmetic and copies ran while one was open for 4% -> 3% of each run, Pallas kernels for 0% -> 14%
where the time goes in v1:
time: 130 us; the launch traced here: 129 us
  Pallas kernels  117 us (90%)
  local copies, waits for them, and re-layouts  7.34 us (6%)
  waiting for transfers between devices  3.07 us (2%)
    pallas_call x1, Pallas kernels, shards(): pl.pallas_call(first_kernel, out_shape=[big, small, sums] + weights, in_s...  52.2 us
    pallas_call x1, Pallas kernels, shards(): pl.pallas_call(functools.partial(second_kernel, scen_total), out_shape=[b...  33.5 us
    pallas_call x2, Pallas kernels, all_sum(): pl.pallas_call(reduce_kernel, out_shape=jax.ShapeDtypeStruct(part.shape,...  29.7 us
    unnamed x5, local copies, waits for them, and re-layouts  5.7 us
    ppermute x1, waiting for transfers between devices, shards(): other = lax.ppermute(prior_states, 'sub', swap)  3.06 us
  transfers between devices with their start and end apart: 2, of which 1 were waited for; matrix products, arithmetic and copies ran while one was open for 3% of the time, Pallas kernels for 14%

profile of v1, /device:TPU:0, one launch (start us, length us, event | category | flops | bytes accessed | tf_op | source)
XLA Modules:
  0.0 129.3 jit_solution(15538500456412123530)
XLA Ops:
  0.6 0.5 collective-permute-start
  1.1 2.4 %copy.14.inv = f32[4,32,16,16]{3,2,1,0:T(8,128)} copy(f32[4,32,16,16]{1,3,2,0:T(8,128)} %param.18) | data formatting | bytes 262144 | tf_op args[7]
  3.6 3.1 %collective-permute-done.other = f32[4,32,48,128]{3,2,1,0:T(8,128)S(1)} collective-permute-done((f32[4,32,48,128]{3,2,1,0:T(8,128)}, f32[4,32,48,128]{3,2,1,0:T(8,128)S(1)}, u32[]{:S(2)}, u32[]{:S(2)}) %collective-permute-start) | collective-permute-done | bytes 3145760 | tf_op jit(solution)/shard_map/ppermute | solution.py:313
  6.6 0.0 copy-start
  6.6 1.7 %copy-done = f32[4,32,48,128]{3,2,1,0:T(8,128)} copy-done((f32[4,32,48,128]{3,2,1,0:T(8,128)}, f32[4,32,48,128]{3,2,1,0:T(8,128)S(1)}, u32[]{:S(2)}) %copy-start) | copy-done | bytes 3145752
  8.3 52.2 %shard_map.130 = (f32[4,32,48,128]{3,2,1,0:T(8,128)}, f32[4,32,16,128]{3,2,1,0:T(8,128)}, f32[16,4,128]{2,1,0:T(4,128)}, bf16[4,32,112,192]{3,2,1,0:T(8,128)(2,1...) custom-call(s32[2,8]{1,0:T(2,128)} %bitcast.3, ...), custom_call_target="tpu_custom_call" | custom-call | tf_op jit(solution)/shard_map/pallas_call | solution.py:314
  60.5 0.4 collective-permute-start.1
  60.9 1.6 %slice.3.before = f32[4,7,16,128]{3,2,1,0:T(8,128)} slice(f32[4,32,16,128]{3,2,1,0:T(8,128)} %get-tuple-element.15), slice={[0:4], [0:7], [0:16], [0:128]} | slice | bytes 458752 | tf_op jit(solution)/shard_map/slice | solution.py:332
  62.5 17.7 %shard_map.131.totals = f32[16,4,128]{2,1,0:T(4,128)} custom-call(f32[16,4,128]{2,1,0:T(4,128)} %get-tuple-element.16.part), custom_call_target="tpu_custom_call" | custom-call | tf_op jit(solution)/shard_map/pallas_call | solution.py:196
  80.3 0.0 collective-permute-done.1.other
  80.3 0.0 copy-start.1
  80.3 1.6 %copy-done.1 = f32[4,32,48,128]{3,2,1,0:T(8,128)} copy-done((f32[4,32,48,128]{3,2,1,0:T(8,128)}, f32[4,32,48,128]{3,2,1,0:T(8,128)S(1)}, u32[]{:S(2)}) %copy-start.1) | copy-done | bytes 3145752
  81.9 33.5 %shard_map.132 = (f32[4,32,48,128]{3,2,1,0:T(8,128)}, f32[4,32,16,128]{3,2,1,0:T(8,128)}, f32[16,4,128]{2,1,0:T(4,128)}, f32[4,7,16,128]{3,2,1,0:T(8,128)}) custom-call(f32[4,32,48,128]{3,2,1,0:T(8,128)} %get-tuple-element.14.own, f32[4,32,48,128]{3,2,1,0:T(8,128)} %copy-done.1, f32[4,32,48,128]{3,2,1,0:T(8,128)} %dist.3, f32[4,7,16,128]{3,2,1,0:T(8,128)} %duals.3, ...), custom_call_target="tpu_custom_call" | custom-call | tf_op jit(solution)/shard_map/pallas_call | solution.py:325
  115.4 12.0 %shard_map.133.totals = f32[16,4,128]{2,1,0:T(4,128)} custom-call(f32[16,4,128]{2,1,0:T(4,128)} %get-tuple-element.24.part), custom_call_target="tpu_custom_call" | custom-call | tf_op jit(solution)/shard_map/pallas_call | solution.py:196
  127.4 1.9 %shard_map.134 = f32[4,7,16,128]{3,2,1,0:T(8,128)} custom-call(f32[4,7,16,128]{3,2,1,0:T(8,128)} %get-tuple-element.23.averaged, s32[6,128]{1,0:T(8,128)} %branches.5, f32[16,4,128]{2,1,0:T(4,128)} %shard_map.133.totals), custom_call_target="tpu_custom_call" | custom-call | tf_op jit(solution)/shard_map/pallas_call | solution.py:334
Async XLA Ops:
  0.6 6.0 %collective-permute-start = (f32[4,32,48,128]{3,2,1,0:T(8,128)}, f32[4,32,48,128]{3,2,1,0:T(8,128)S(1)}, u32[]{:S(2)}, u32[]{:S(2)}) collective-permute-start(f32[4,32,48,128]{3,2,1,0:T(8,128)} %own.1), channel_id=1, source_target_pairs={{1,0},{0,1},{3,2},{2,3},{5,4},{4,5},{7,6},{6,7},{9,8},{8,9},{11,10... | collective-permute-start | bytes 9437192 | tf_op jit(solution)/shard_map/ppermute | solution.py:313
  6.6 1.7 %copy-start = (f32[4,32,48,128]{3,2,1,0:T(8,128)}, f32[4,32,48,128]{3,2,1,0:T(8,128)S(1)}, u32[]{:S(2)}) copy-start(f32[4,32,48,128]{3,2,1,0:T(8,128)S(1)} %collective-permute-done.other) | copy-start | bytes 9437188
  60.5 19.8 %collective-permute-start.1 = (f32[4,32,48,128]{3,2,1,0:T(8,128)}, f32[4,32,48,128]{3,2,1,0:T(8,128)S(1)}, u32[]{:S(2)}, u32[]{:S(2)}) collective-permute-start(f32[4,32,48,128]{3,2,1,0:T(8,128)} %get-tuple-element.14.own), channel_id=1, source_target_pairs={{1,0},{0,1},{3,2},{2,3},{5,4},{4,5},{7,6},{6,7},{9,8},{8,9},{11,10... | collective-permute-start | bytes 9437192 | tf_op jit(solution)/shard_map/ppermute | solution.py:323
  80.3 1.6 %copy-start.1 = (f32[4,32,48,128]{3,2,1,0:T(8,128)}, f32[4,32,48,128]{3,2,1,0:T(8,128)S(1)}, u32[]{:S(2)}) copy-start(f32[4,32,48,128]{3,2,1,0:T(8,128)S(1)} %collective-permute-done.1.other) | copy-start | bytes 9437188

commit v2 on v1

--- a/solution.py
+++ b/solution.py
@@ -61,6 +61,16 @@
         wb[m, t] = wide(jnp.concatenate([front.T, bottom], axis=0))
 
 
+def stepped(count, step, carry, each=4):
+    def several(k, c):
+        for r in range(each):
+            c = step(k * each + r, c)
+        return c
+
+    carry = lax.fori_loop(0, count // each, several, carry)
+    return lax.fori_loop(count // each * each, count, step, carry)
+
+
 def couple(subs, own_first, other_first, neigh, coup, cx):
     nb, nx, ncp = coup.shape[1:]
     for side, first in enumerate((own_first, other_first)):
@@ -112,7 +122,7 @@
 
     zero = tuple(jnp.zeros((nx, s), F32) for _ in range(subs))
     carry = (zero, grow(steps - 1))
-    carry = lax.fori_loop(0, steps - robust, lambda k, c: back(steps - 1 - k, c, False), carry)
+    carry = stepped(steps - robust, lambda k, c: back(steps - 1 - k, c, False), carry)
     carry = lax.fori_loop(0, robust, lambda k, c: back(robust - 1 - k, c, True), carry)
 
     def ahead(t, x):
@@ -240,7 +250,7 @@
     n_sub = coup.shape[0] // subs
     me = lax.axis_index("sub")
     couple(subs, me * subs, lax.rem(me + 1, n_sub) * subs, neigh, coup, cx)
-    each = 2 if steps % 2 == 0 else 1
+    each = 4 if steps % 4 == 0 else 1
 
     def prep(k, c):
         prepare([k * each + r for r in range(each)], dyn, act_t, ctg, inv, wb, wf, wp)
@@ -248,7 +258,7 @@
 
     lax.fori_loop(0, steps // each, prep, 0)
     step, x = sweep(own, other, dist, duals, init, wb, wf, wp, cx, drive, offs, states, controls)
-    lax.fori_loop(0, steps, step, x)
+    stepped(steps, step, x)
     averaged = [gathered(controls, duals, t) for t in range(robust)]
     put(sums, node_sums(averaged, node_ids(branches[...]), sums.shape[2]))
 
@@ -267,7 +277,7 @@
             duals_now[i, t] = now
             linear[i, t] = now - c
     step, x = sweep(own, other, dist, linear, init, wb, wf, wp, cx, drive, offs, states, controls)
-    lax.fori_loop(0, steps, step, x)
+    stepped(steps, step, x)
     averaged = []
     for t in range(robust):
         v = gathered(controls, duals_now, t)

time: 130 us -> 126 us (0.969)
  Pallas kernels: 117 us -> 114 us
    pallas_call x1, Pallas kernels: 52.2 us -> 48.8 us  [shards(): pl.pallas_call(first_kernel, out_shape=[big, small, sums] + weights, in_s...]
where the time goes in v2:
time: 126 us
  Pallas kernels  114 us (90%)
  local copies, waits for them, and re-layouts  7.34 us (6%)
  waiting for transfers between devices  3.07 us (2%)
    pallas_call x1, Pallas kernels, shards(): pl.pallas_call(first_kernel, out_shape=[big, small, sums] + weights, in_s...  48.8 us
    pallas_call x1, Pallas kernels, shards(): pl.pallas_call(functools.partial(second_kernel, scen_total), out_shape=[b...  33.3 us
    pallas_call x2, Pallas kernels, all_sum(): pl.pallas_call(reduce_kernel, out_shape=jax.ShapeDtypeStruct(part.shape,...  29.7 us
    unnamed x5, local copies, waits for them, and re-layouts  5.7 us
    ppermute x1, waiting for transfers between devices, shards(): other = lax.ppermute(prior_states, 'sub', swap)  3.06 us
  transfers between devices with their start and end apart: 2, of which 1 were waited for; matrix products, arithmetic and copies ran while one was open for 3% of the time, Pallas kernels for 14%

profile of v2, /device:TPU:0, one launch (start us, length us, event | category | flops | bytes accessed | tf_op | source)
XLA Modules:
  0.0 125.7 jit_solution(16743960163365281887)
XLA Ops:
  0.6 0.5 collective-permute-start
  1.1 2.4 %copy.14.inv = f32[4,32,16,16]{3,2,1,0:T(8,128)} copy(f32[4,32,16,16]{1,3,2,0:T(8,128)} %param.18) | data formatting | bytes 262144 | tf_op args[7]
  3.6 3.1 %collective-permute-done.other = f32[4,32,48,128]{3,2,1,0:T(8,128)S(1)} collective-permute-done((f32[4,32,48,128]{3,2,1,0:T(8,128)}, f32[4,32,48,128]{3,2,1,0:T(8,128)S(1)}, u32[]{:S(2)}, u32[]{:S(2)}) %collective-permute-start) | collective-permute-done | bytes 3145760 | tf_op jit(solution)/shard_map/ppermute | solution.py:323
  6.6 0.0 copy-start
  6.6 1.7 %copy-done = f32[4,32,48,128]{3,2,1,0:T(8,128)} copy-done((f32[4,32,48,128]{3,2,1,0:T(8,128)}, f32[4,32,48,128]{3,2,1,0:T(8,128)S(1)}, u32[]{:S(2)}) %copy-start) | copy-done | bytes 3145752
  8.3 48.8 %shard_map.130 = (f32[4,32,48,128]{3,2,1,0:T(8,128)}, f32[4,32,16,128]{3,2,1,0:T(8,128)}, f32[16,4,128]{2,1,0:T(4,128)}, bf16[4,32,112,192]{3,2,1,0:T(8,128)(2,1...) custom-call(s32[2,8]{1,0:T(2,128)} %bitcast.3, ...), custom_call_target="tpu_custom_call" | custom-call | tf_op jit(solution)/shard_map/pallas_call | solution.py:324
  57.1 0.4 collective-permute-start.1
  57.5 1.6 %slice.3.before = f32[4,7,16,128]{3,2,1,0:T(8,128)} slice(f32[4,32,16,128]{3,2,1,0:T(8,128)} %get-tuple-element.15), slice={[0:4], [0:7], [0:16], [0:128]} | slice | bytes 458752 | tf_op jit(solution)/shard_map/slice | solution.py:342
  59.1 17.7 %shard_map.131.totals = f32[16,4,128]{2,1,0:T(4,128)} custom-call(f32[16,4,128]{2,1,0:T(4,128)} %get-tuple-element.16.part), custom_call_target="tpu_custom_call" | custom-call | tf_op jit(solution)/shard_map/pallas_call | solution.py:206
  76.9 0.0 collective-permute-done.1.other
  76.9 0.0 copy-start.1
  76.9 1.6 %copy-done.1 = f32[4,32,48,128]{3,2,1,0:T(8,128)} copy-done((f32[4,32,48,128]{3,2,1,0:T(8,128)}, f32[4,32,48,128]{3,2,1,0:T(8,128)S(1)}, u32[]{:S(2)}) %copy-start.1) | copy-done | bytes 3145752
  78.5 33.3 %shard_map.132 = (f32[4,32,48,128]{3,2,1,0:T(8,128)}, f32[4,32,16,128]{3,2,1,0:T(8,128)}, f32[16,4,128]{2,1,0:T(4,128)}, f32[4,7,16,128]{3,2,1,0:T(8,128)}) custom-call(f32[4,32,48,128]{3,2,1,0:T(8,128)} %get-tuple-element.14.own, f32[4,32,48,128]{3,2,1,0:T(8,128)} %copy-done.1, f32[4,32,48,128]{3,2,1,0:T(8,128)} %dist.3, f32[4,7,16,128]{3,2,1,0:T(8,128)} %duals.3, ...), custom_call_target="tpu_custom_call" | custom-call | tf_op jit(solution)/shard_map/pallas_call | solution.py:335
  111.8 12.0 %shard_map.133.totals = f32[16,4,128]{2,1,0:T(4,128)} custom-call(f32[16,4,128]{2,1,0:T(4,128)} %get-tuple-element.24.part), custom_call_target="tpu_custom_call" | custom-call | tf_op jit(solution)/shard_map/pallas_call | solution.py:206
  123.8 1.9 %shard_map.134 = f32[4,7,16,128]{3,2,1,0:T(8,128)} custom-call(f32[4,7,16,128]{3,2,1,0:T(8,128)} %get-tuple-element.23.averaged, s32[6,128]{1,0:T(8,128)} %branches.5, f32[16,4,128]{2,1,0:T(4,128)} %shard_map.133.totals), custom_call_target="tpu_custom_call" | custom-call | tf_op jit(solution)/shard_map/pallas_call | solution.py:344
Async XLA Ops:
  0.6 6.0 %collective-permute-start = (f32[4,32,48,128]{3,2,1,0:T(8,128)}, f32[4,32,48,128]{3,2,1,0:T(8,128)S(1)}, u32[]{:S(2)}, u32[]{:S(2)}) collective-permute-start(f32[4,32,48,128]{3,2,1,0:T(8,128)} %own.1), channel_id=1, source_target_pairs={{1,0},{0,1},{3,2},{2,3},{5,4},{4,5},{7,6},{6,7},{9,8},{8,9},{11,10... | collective-permute-start | bytes 9437192 | tf_op jit(solution)/shard_map/ppermute | solution.py:323
  6.6 1.7 %copy-start = (f32[4,32,48,128]{3,2,1,0:T(8,128)}, f32[4,32,48,128]{3,2,1,0:T(8,128)S(1)}, u32[]{:S(2)}) copy-start(f32[4,32,48,128]{3,2,1,0:T(8,128)S(1)} %collective-permute-done.other) | copy-start | bytes 9437188
  57.1 19.8 %collective-permute-start.1 = (f32[4,32,48,128]{3,2,1,0:T(8,128)}, f32[4,32,48,128]{3,2,1,0:T(8,128)S(1)}, u32[]{:S(2)}, u32[]{:S(2)}) collective-permute-start(f32[4,32,48,128]{3,2,1,0:T(8,128)} %get-tuple-element.14.own), channel_id=1, source_target_pairs={{1,0},{0,1},{3,2},{2,3},{5,4},{4,5},{7,6},{6,7},{9,8},{8,9},{11,10... | collective-permute-start | bytes 9437192 | tf_op jit(solution)/shard_map/ppermute | solution.py:333
  76.9 1.6 %copy-start.1 = (f32[4,32,48,128]{3,2,1,0:T(8,128)}, f32[4,32,48,128]{3,2,1,0:T(8,128)S(1)}, u32[]{:S(2)}) copy-start(f32[4,32,48,128]{3,2,1,0:T(8,128)S(1)} %collective-permute-done.1.other) | copy-start | bytes 9437188
